TPU v7x, 256 devices: a whole 4x4x8 slice. The times are simulated.
256 devices in a mesh: visit: 32 (over y, z), tile: 8 (over x, core).
Axes of the slice: x: 4, y: 4, z: 8, core: 2. Of those that a mesh axis runs over, the one named last changes fastest.
Arguments:
- visit_image: bfloat16 [32, 2048, 2048], P('visit', 'tile'), may hold values from -6 to 6
- good_mask: int32 [32, 2048, 2048], P('visit', 'tile'), may hold values 0 or 1
- basis_rows: float32 [27, 21], replicated, may hold values from -1.25 to 1.25
- basis_cols: float32 [27, 21], replicated, may hold values from -1.25 to 1.25
- visit_coeff: float32 [32, 27], P('visit'), may hold values from -1.25 to 1.25
- visit_weight: float32 [32], P('visit'), may hold values from 0.25 to 4
- col_offset: int32 [32], P('visit'), may hold values from -64 to 64
- patch_of: int32 [32, 1], replicated, may hold values from 0 to 7
- new_image: bfloat16 [32, 2048, 2048], P('visit', 'tile'), may hold values from -6 to 6
- new_coeff: float32 [32, 27], P('visit'), may hold values from -1.25 to 1.25
- new_patch: int32 [32, 1], replicated, may hold values from 0 to 7
Outputs:
- coadd: bfloat16 [8, 8, 256, 2048], P(None, 'tile', 'visit')
- difference: float32 [32, 2048, 2048], P('visit', 'tile')
Inputs may be any that keep to these rules, and one draw needn't show every extreme that they name: `patch_of`: every one of the 8 patches is intersected by at least one visit. `new_patch`: every one of the 8 patches lies under at least one new visit.
All inputs are finite; a program needn't handle non-finite values. No bound on the sum of `good_mask` on one device may be relied on, other than what follows from the above.
Results may differ from a plain program's by a relative error of at most 0.007.
Values may be sent and summed in bfloat16 or wider, within the bound.
No kernel may reach another device: no remote copies, remote signals or barrier semaphores. Data moves between devices by JAX's collectives and lax.ppermute only.
A program may use at most 128 MiB of HBM per device.

v0:
```python
import jax
import jax.numpy as jnp
from jax import lax
from jax.sharding import PartitionSpec as P

KS = 21
PATCHES = 8
OFF = 64


def with_halo(block, sides, width):
    for axis, dim in sides:
        count = lax.axis_size(axis)
        forward = [(i, i + 1) for i in range(count - 1)]
        backward = [(target, source) for source, target in forward]
        low = lax.ppermute(
            lax.slice_in_dim(block, block.shape[dim] - width, None, axis=dim), axis, forward
        )
        high = lax.ppermute(lax.slice_in_dim(block, 0, width, axis=dim), axis, backward)
        block = jnp.concatenate([low, block, high], axis=dim)
    return block


def build_kernel(coefficients, basis_rows, basis_cols):
    summed = jnp.sum(
        coefficients[:, None, None] * basis_rows[:, :, None] * basis_cols[:, None, :], axis=0
    )
    return summed.astype(jnp.bfloat16)


def toeplitz(kernel, block_size):
    span = block_size + KS - 1
    spread = jnp.arange(span)[:, None] - jnp.arange(block_size)[None, :]
    onehot = (spread[None, :, :] == jnp.arange(KS)[:, None, None]).astype(jnp.bfloat16)
    product = jnp.dot(
        kernel, onehot.reshape(KS, span * block_size), preferred_element_type=jnp.float32
    )
    return product.reshape(KS, span, block_size).astype(jnp.bfloat16)


def convolve(extended, kernel):
    halfwidth = KS // 2
    height = extended.shape[0] - (KS - 1)
    columns = extended.shape[1]
    block_size = 128
    number = columns // block_size
    padded = jnp.pad(extended, ((0, 0), (halfwidth, block_size - halfwidth)))
    blocks = padded.reshape(extended.shape[0], number + 1, block_size)
    windows = jnp.concatenate([blocks[:, :-1], blocks[:, 1:, : KS - 1]], axis=2)
    table = toeplitz(kernel, block_size)
    running = jnp.zeros((height, number, block_size), jnp.float32)
    for shift_row in range(KS):
        running = running + jnp.einsum(
            "rgk,ko->rgo",
            windows[shift_row : shift_row + height],
            table[shift_row],
            preferred_element_type=jnp.float32,
        )
    return running.reshape(height, columns)


def per_device(
    visit_image,
    good_mask,
    basis_rows,
    basis_cols,
    visit_coeff,
    visit_weight,
    col_offset,
    patch_of,
    new_image,
    new_coeff,
    new_patch,
):
    halfwidth = KS // 2
    extended = with_halo(visit_image[0], (("tile", 0),), halfwidth)
    matched = convolve(extended, build_kernel(visit_coeff[0], basis_rows, basis_cols))
    height, columns = matched.shape
    first_col = OFF - col_offset[0]
    placed = lax.dynamic_slice_in_dim(jnp.pad(matched, ((0, 0), (OFF, OFF))), first_col, columns, 1)
    inside = lax.dynamic_slice_in_dim(
        jnp.pad(good_mask[0].astype(jnp.float32), ((0, 0), (OFF, OFF))), first_col, columns, 1
    )
    coverage = visit_weight[0] * inside
    weighted = (placed * coverage).astype(jnp.bfloat16)
    cover_rounded = coverage.astype(jnp.bfloat16)
    owners = lax.axis_size("visit")
    slice_rows = height // owners
    visit_onehot = (patch_of[:, 0][None, :] == jnp.arange(PATCHES)[:, None]).astype(jnp.bfloat16)
    outgoing = (
        weighted.reshape(owners, slice_rows, columns),
        cover_rounded.reshape(owners, slice_rows, columns),
    )
    weighted_rows = lax.all_to_all(outgoing[0], "visit", split_axis=0, concat_axis=0, tiled=True)
    cover_rows = lax.all_to_all(outgoing[1], "visit", split_axis=0, concat_axis=0, tiled=True)
    numerator = jnp.einsum(
        "pv,vsw->psw", visit_onehot, weighted_rows, preferred_element_type=jnp.float32
    )
    denominator = jnp.einsum(
        "pv,vsw->psw", visit_onehot, cover_rows, preferred_element_type=jnp.float32
    )
    coadd = (numerator / jnp.maximum(denominator, 1.0)).astype(jnp.bfloat16)
    gathered = lax.all_gather(coadd, "visit", axis=1, tiled=True)
    patch_index = lax.dynamic_index_in_dim(
        new_patch[:, 0], lax.axis_index("visit"), 0, keepdims=False
    )
    template = lax.dynamic_index_in_dim(gathered, patch_index, 0, keepdims=False)
    template_ext = with_halo(template, (("tile", 0),), halfwidth)
    difference = new_image[0].astype(jnp.float32) - convolve(
        template_ext, build_kernel(new_coeff[0], basis_rows, basis_cols)
    )
    return (coadd[:, None], difference[None])


def solution(mesh):
    return jax.shard_map(
        per_device,
        mesh=mesh,
        in_specs=(
            P("visit", "tile", None),
            P("visit", "tile", None),
            P(),
            P(),
            P("visit", None),
            P("visit"),
            P("visit"),
            P(),
            P("visit", "tile", None),
            P("visit", None),
            P(),
        ),
        out_specs=(P(None, "tile", "visit", None), P("visit", "tile", None)),
        check_vma=False,
    )
```

profile of v0, /device:TPU:1, one launch (start us, length us, event | category | flops | bytes accessed | tf_op | source)
XLA Modules:
  0.0 335.7 jit_solution(6419589440406265364)
XLA Ops:
  8.1 4.5 %collective-permute-start = (bf16[10,2048]{1,0:T(8,128)(2,1)S(1)}, bf16[10,2048]{1,0:T(8,128)(2,1)S(1)}, u32[]{:S(2)}, u32[]{:S(2)}) collective-permute-start(bf16[10,2048]{1,0:T(8,128)(2,1)S(1)} %get-tuple-element.16), channel_id=1, source_target_pairs={{0,1},{1,2},{2,3},{3,4},{4,5},{5,6},{6,7},{8,9},{9,10},{10,11},{11... | collective-permute-start | bytes 122888 | tf_op jit(solution)/shard_map/ppermute | solution.py:16
  16.7 2.1 fusion.356
  27.3 2.1 fusion.110
  29.5 2.1 fusion.113
  31.6 2.1 fusion.116
  33.7 2.1 fusion.119
  35.8 2.1 fusion.122
  37.9 2.2 fusion.125
  40.0 2.0 fusion.80
  42.1 2.0 fusion.83
  44.1 2.1 fusion.86
  46.2 2.1 fusion.89
  48.3 2.1 fusion.92
  50.4 2.1 fusion.95
  52.6 2.1 fusion.98
  54.7 2.3 fusion.128
  57.0 2.1 fusion.71
  60.8 2.1 fusion.77
  62.9 13.9 %add_add_fusion.1 = f32[256,16,128]{0,2,1:T(8,128)} fusion(f32[256,16,128]{0,2,1:T(8,128)} %fusion.71, f32[256,16,128]{0,2,1:T(8,128)} %fusion.128, f32[256,16,128]{0,2,1:T(8,128)} %fusion.125, f32[256,16,128]{0,2,1:T(8,128)} %fusion.122, f32[256,16,128]{0,2,1:T(8,128)} %fusion.119, f32[256,16,128]{0,2,1:T(8,128)} %fusion.116, ...), kind=kOutput, calls=%fused_computation.51 | convolution fusion | flops 168099840 | bytes 45385216 | tf_op jit(solution)/shard_map/rgk,ko->rgo/dot_general | solution.py:53
  76.9 3.1 copy.44
  79.9 4.3 %fusion.172 = (bf16[32,8,2048]{2,1,0:T(8,128)(2,1)}, bf16[32,8,2048]{2,1,0:T(8,128)(2,1)S(1)}) fusion(s32[]{:T(128)S(6)} %select_n.12, f32[256,2048]{1,0:T(8,128)S(1)} %copy-done.2, f32[]{:T(128)} %bitcast.166, f32[256,2048]{1,0:T(8,128)} %copy.44), kind=kLoop, calls=%fused_computation.184 | loop fusion | flops 2621440 | bytes 6291464 | tf_op jit(solution)/shard_map/reshape | solution.py:92
  84.2 38.8 %all_to_all.10 = bf16[32,8,2048]{2,1,0:T(8,128)(2,1)S(1)} all-to-all(bf16[32,8,2048]{2,1,0:T(8,128)(2,1)S(1)} %get-tuple-element.13), channel_id=1, replica_groups=mesh['visit'=32,'tile'=8] {'visit'}, dimensions={0} | all-to-all | bytes 2097152 | tf_op jit(solution)/shard_map/all_to_all | solution.py:94
  123.0 4.8 %all-to-all-start.1 = ((bf16[32,8,2048]{2,1,0:T(8,128)(2,1)}), bf16[32,8,2048]{2,1,0:T(8,128)(2,1)S(1)}, u32[]{:S(2)}, u32[]{:S(2)}) async-start(bf16[32,8,2048]{2,1,0:T(8,128)(2,1)} %get-tuple-element.12), calls=%async_computation.1 | async-start | bytes 2097152 | tf_op jit(solution)/shard_map/all_to_all | solution.py:95
  129.4 24.5 %all-to-all-done.1 = bf16[32,8,2048]{2,1,0:T(8,128)(2,1)S(1)} async-done(((bf16[32,8,2048]{2,1,0:T(8,128)(2,1)}), bf16[32,8,2048]{2,1,0:T(8,128)(2,1)S(1)}, u32[]{:S(2)}, u32[]{:S(2)}) %all-to-all-start.1) | async-done | bytes 1048608 | tf_op jit(solution)/shard_map/all_to_all | solution.py:95
  158.8 2.2 fusion.354
  161.0 93.0 %all-gather.2.cloned.1.call-done = bf16[8,256,2048]{2,0,1:T(8,128)(2,1)} async-done(((bf16[8,8,2048]{2,0,1:T(8,128)(2,1)}), bf16[8,256,2048]{2,0,1:T(8,128)(2,1)}) %all-gather.2.cloned.1.call-update) | async-done | bytes 8388624 | tf_op jit(solution)/shard_map/all_gather | solution.py:103
  253.9 5.7 %constant_dynamic-slice_fusion = bf16[1,256,2048]{2,0,1:T(2,128)(2,1)S(1)} fusion(bf16[8,256,2048]{2,0,1:T(8,128)(2,1)} %all-gather.2.cloned.1.call-done, s32[]{:T(128)S(6)} %select_n.14), kind=kLoop, calls=%fused_computation.332 | loop fusion | bytes 2097156 | tf_op jit(solution)/shard_map/jit(dynamic_index_in_dim)/dynamic_slice | solution.py:107
  260.3 4.1 %collective-permute-start.2 = (bf16[10,2048]{1,0:T(8,128)(2,1)S(1)}, bf16[10,2048]{1,0:T(8,128)(2,1)S(1)}, u32[]{:S(2)}, u32[]{:S(2)}) collective-permute-start(bf16[10,2048]{1,0:T(8,128)(2,1)S(1)} %get-tuple-element.14), channel_id=1, source_target_pairs={{0,1},{1,2},{2,3},{3,4},{4,5},{5,6},{6,7},{8,9},{9,10},{10,11},{11... | collective-permute-start | bytes 122888 | tf_op jit(solution)/shard_map/ppermute | solution.py:16
  267.8 2.1 collective-permute-done.3
  274.5 2.1 fusion.23
  276.6 2.1 fusion.26
  278.7 2.1 fusion.29
  280.8 2.1 fusion.32
  283.0 2.1 fusion.35
  285.1 2.2 fusion.38
  287.2 2.0 fusion.41
  289.3 2.0 fusion.44
  291.3 2.1 fusion.47
  293.4 2.1 fusion.50
  295.5 2.1 fusion.53
  297.6 2.1 fusion.56
  299.8 2.1 fusion.59
  301.8 2.2 fusion.62
  304.0 2.3 fusion.65
  306.3 2.1 fusion.68
  308.4 2.1 fusion.11
  310.5 14.4 %add_add_fusion = f32[256,16,128]{0,2,1:T(8,128)} fusion(f32[256,16,128]{0,2,1:T(8,128)} %fusion.11, f32[256,16,128]{0,2,1:T(8,128)} %fusion.68, f32[256,16,128]{0,2,1:T(8,128)} %fusion.65, f32[256,16,128]{0,2,1:T(8,128)} %fusion.62, f32[256,16,128]{0,2,1:T(8,128)} %fusion.59, f32[256,16,128]{0,2,1:T(8,128)} %fusion.56, f32[256,16,128]{0,2,1:T(8,128)} %fusion.53, ...), kind=kOutput, calls=%fused_computation.48 | convolution fusion | flops 168099840 | bytes 45385216 | tf_op jit(solution)/shard_map/rgk,ko->rgo/dot_general | solution.py:53
  324.9 2.0 copy.49
  (129 shorter events, 28.7 us)
Async XLA Ops:
  7.2 148.6 %copy-start = (s32[32,1]{0,1:T(1,128)S(1)}, s32[32,1]{0,1:T(1,128)}, u32[]{:S(2)}) copy-start(s32[32,1]{0,1:T(1,128)} %param.21) | copy-start | bytes 388
  8.1 14.4 %collective-permute-start = (bf16[10,2048]{1,0:T(8,128)(2,1)S(1)}, bf16[10,2048]{1,0:T(8,128)(2,1)S(1)}, u32[]{:S(2)}, u32[]{:S(2)}) collective-permute-start(bf16[10,2048]{1,0:T(8,128)(2,1)S(1)} %get-tuple-element.16), channel_id=1, source_target_pairs={{0,1},{1,2},{2,3},{3,4},{4,5},{5,6},{6,7},{8,9},{9,10},{10,11},{11... | collective-permute-start | bytes 122888 | tf_op jit(solution)/shard_map/ppermute | solution.py:16
  12.6 9.9 %collective-permute-start.1 = (bf16[10,2048]{1,0:T(8,128)(2,1)S(1)}, bf16[10,2048]{1,0:T(8,128)(2,1)S(1)}, u32[]{:S(2)}, u32[]{:S(2)}) collective-permute-start(bf16[10,2048]{1,0:T(8,128)(2,1)S(1)} %get-tuple-element.17), channel_id=1, source_target_pairs={{1,0},{2,1},{3,2},{4,3},{5,4},{6,5},{7,6},{9,8},{10,9},{11,10},{12... | collective-permute-start | bytes 122888 | tf_op jit(solution)/shard_map/ppermute | solution.py:19
  16.2 2.6 copy-start.3
  18.8 3.7 %copy-start.4 = (bf16[1,256,2048]{2,1,0:T(8,128)(2,1)S(1)}, bf16[1,256,2048]{2,1,0:T(8,128)(2,1)}, u32[]{:S(2)}) copy-start(bf16[1,256,2048]{2,1,0:T(8,128)(2,1)} %param.11) | copy-start | bytes 3145732
  25.6 0.9 copy-start.42
  27.3 2.1 copy-start.40
  29.5 2.1 copy-start.39
  31.6 2.1 copy-start.38
  33.7 2.1 copy-start.37
  35.8 2.1 copy-start.36
  37.9 2.2 copy-start.35
  40.0 2.0 copy-start.34
  42.1 2.1 copy-start.33
  44.1 2.1 copy-start.32
  46.2 2.1 copy-start.31
  48.3 2.1 copy-start.30
  50.4 2.1 copy-start.29
  52.6 2.1 copy-start.28
  54.7 2.3 copy-start.27
  57.0 2.1 copy-start.8
  59.1 1.8 copy-start.7
  76.8 3.1 copy-start.2
  84.2 43.9 %copy-start.43 = (s32[32,1]{0,1:T(1,128)S(1)}, s32[32,1]{0,1:T(1,128)}, u32[]{:S(2)}) copy-start(s32[32,1]{0,1:T(1,128)} %param.18) | copy-start | bytes 388
  123.0 30.8 %all-to-all-start.1 = ((bf16[32,8,2048]{2,1,0:T(8,128)(2,1)}), bf16[32,8,2048]{2,1,0:T(8,128)(2,1)S(1)}, u32[]{:S(2)}, u32[]{:S(2)}) async-start(bf16[32,8,2048]{2,1,0:T(8,128)(2,1)} %get-tuple-element.12), calls=%async_computation.1 | async-start | bytes 2097152 | tf_op jit(solution)/shard_map/all_to_all | solution.py:95
  127.9 126.0 %all-gather.2.cloned.1.call-start = ((), (), s32[]{:S(2)}) async-start(), calls=%async_computation.2 | async-start | bytes 8650752 | tf_op jit(solution)/shard_map/all_gather | solution.py:103
  259.6 6.8 %copy-start.6 = (bf16[8,8,2048]{2,0,1:T(8,128)(2,1)S(1)}, bf16[8,8,2048]{2,0,1:T(8,128)(2,1)}, u32[]{:S(2)}) copy-start(bf16[8,8,2048]{2,0,1:T(8,128)(2,1)} %fusion.1) | copy-start | bytes 786436
  260.3 7.6 %collective-permute-start.2 = (bf16[10,2048]{1,0:T(8,128)(2,1)S(1)}, bf16[10,2048]{1,0:T(8,128)(2,1)S(1)}, u32[]{:S(2)}, u32[]{:S(2)}) collective-permute-start(bf16[10,2048]{1,0:T(8,128)(2,1)S(1)} %get-tuple-element.14), channel_id=1, source_target_pairs={{0,1},{1,2},{2,3},{3,4},{4,5},{5,6},{6,7},{8,9},{9,10},{10,11},{11... | collective-permute-start | bytes 122888 | tf_op jit(solution)/shard_map/ppermute | solution.py:16
  264.3 5.6 %collective-permute-start.3 = (bf16[10,2048]{1,0:T(8,128)(2,1)S(1)}, bf16[10,2048]{1,0:T(8,128)(2,1)S(1)}, u32[]{:S(2)}, u32[]{:S(2)}) collective-permute-start(bf16[10,2048]{1,0:T(8,128)(2,1)S(1)} %get-tuple-element.15), channel_id=1, source_target_pairs={{1,0},{2,1},{3,2},{4,3},{5,4},{6,5},{7,6},{9,8},{10,9},{11,10},{12... | collective-permute-start | bytes 122888 | tf_op jit(solution)/shard_map/ppermute | solution.py:19
  272.8 0.9 copy-start.26
  274.5 2.1 copy-start.24
  276.6 2.1 copy-start.23
  278.7 2.1 copy-start.22
  280.8 2.1 copy-start.21
  283.0 2.1 copy-start.20
  285.0 2.2 copy-start.19
  287.2 2.0 copy-start.18
  289.3 2.1 copy-start.17
  291.3 2.1 copy-start.16
  293.4 2.1 copy-start.15
  295.5 2.1 copy-start.14
  297.6 2.1 copy-start.13
  299.8 2.1 copy-start.12
  301.8 2.2 copy-start.11
  304.0 2.3 copy-start.10
  306.3 2.1 copy-start.9
  324.9 2.0 copy-start.5
  324.9 3.6 %copy-start.1 = (s32[32,1]{0,1:T(1,128)S(1)}, s32[32,1]{0,1:T(1,128)}, u32[]{:S(2)}) copy-start(s32[32,1]{0,1:T(1,128)} %param.21) | copy-start | bytes 388
  (2 other events, 1.8 us)
Sparse Core Ops, SparseCore 0:
  155.9 97.9 all-gather.1
where the time goes:
time: 339 us; the launch traced here: 336 us
  waiting for transfers between devices  120 us (35%)
  matrix products  108 us (32%)
  blocking collectives  38.8 us (11%)
  local copies, waits for them, and re-layouts  24.2 us (7%)
  between operations  18 us (5%)
  starting transfers between devices  17.5 us (5%)
  other arithmetic  9.66 us (3%)
    dot_general x42, matrix products, convolve(): jnp.einsum('rgk,ko->rgo', windows[shift_row:shift_row + height], table[sh...  104 us
    all_gather x1, waiting for transfers between devices, per_device(): gathered = lax.all_gather(coadd, 'visit', axis=1, tiled=True)  93 us
    all_to_all x1, blocking collectives, per_device(): lax.all_to_all(outgoing[0], 'visit', split_axis=0, concat_axis=0, tiled=T...  38.8 us
    all_to_all x1, waiting for transfers between devices, per_device(): lax.all_to_all(outgoing[1], 'visit', split_axis=0, concat_axis=0, tiled=T...  24.5 us
    ppermute x2, starting transfers between devices, with_halo(): lax.ppermute(lax.slice_in_dim(block, block.shape[dim] - width, None, axis...  8.58 us
  transfers between devices with their start and end apart: 6, of which 3 were waited for; matrix products, arithmetic and copies ran while one was open for 4% of the time, Pallas kernels for 0%

commit v1 on v0

--- a/solution.py
+++ b/solution.py
@@ -100,7 +100,9 @@
         "pv,vsw->psw", visit_onehot, cover_rows, preferred_element_type=jnp.float32
     )
     coadd = (numerator / jnp.maximum(denominator, 1.0)).astype(jnp.bfloat16)
-    gathered = lax.all_gather(coadd, "visit", axis=1, tiled=True)
+    gathered = jnp.concatenate(
+        lax.all_to_all(jnp.stack([coadd] * lax.axis_size("visit")), "visit", 0, 0), axis=1
+    )
     patch_index = lax.dynamic_index_in_dim(
         new_patch[:, 0], lax.axis_index("visit"), 0, keepdims=False
     )

time: 339 us -> 439 us (1.29)
  the two profiles are of different devices: /device:TPU:1 before, /device:TPU:33 now
where the time goes in v1:
time: 439 us; the launch traced here: 435 us
  waiting for transfers between devices  222 us (51%)
  matrix products  107 us (24%)
  blocking collectives  38.6 us (9%)
  local copies, waits for them, and re-layouts  32.2 us (7%)
  starting transfers between devices  20 us (5%)
  other arithmetic  9.7 us (2%)
  between operations  4.53 us (1%)
    all_to_all x1, waiting for transfers between devices, per_device(): lax.all_to_all(jnp.stack([coadd] * lax.axis_size('visit')), 'visit', 0, 0)  193 us
    dot_general x42, matrix products, convolve(): jnp.einsum('rgk,ko->rgo', windows[shift_row:shift_row + height], table[sh...  104 us
    all_to_all x1, blocking collectives, per_device(): lax.all_to_all(outgoing[0], 'visit', split_axis=0, concat_axis=0, tiled=T...  38.6 us
    all_to_all x1, waiting for transfers between devices, per_device(): lax.all_to_all(outgoing[1], 'visit', split_axis=0, concat_axis=0, tiled=T...  27.4 us
  transfers between devices with their start and end apart: 6, of which 3 were waited for; matrix products, arithmetic and copies ran while one was open for 3% of the time, Pallas kernels for 0%

profile of v1, /device:TPU:33, one launch (start us, length us, event | category | flops | bytes accessed | tf_op | source)
XLA Modules:
  0.0 434.8 jit_solution(13119818219933887852)
XLA Ops:
  1.5 3.7 collective-permute-start
  9.3 2.1 fusion.356
  20.0 2.1 fusion.110
  22.1 2.1 fusion.113
  24.2 2.1 fusion.116
  26.3 2.1 fusion.119
  28.4 2.1 fusion.122
  30.5 2.2 fusion.125
  32.6 2.0 fusion.80
  34.7 2.1 fusion.83
  36.8 2.1 fusion.86
  38.9 2.1 fusion.89
  41.0 2.1 fusion.92
  43.1 2.1 fusion.95
  45.2 2.1 fusion.98
  47.3 2.3 fusion.128
  49.6 2.1 fusion.71
  53.5 2.1 fusion.77
  55.6 13.9 %add_add_fusion.1 = f32[256,16,128]{0,2,1:T(8,128)} fusion(f32[256,16,128]{0,2,1:T(8,128)} %fusion.71, f32[256,16,128]{0,2,1:T(8,128)} %fusion.128, f32[256,16,128]{0,2,1:T(8,128)} %fusion.125, f32[256,16,128]{0,2,1:T(8,128)} %fusion.122, f32[256,16,128]{0,2,1:T(8,128)} %fusion.119, f32[256,16,128]{0,2,1:T(8,128)} %fusion.116, ...), kind=kOutput, calls=%fused_computation.52 | convolution fusion | flops 168099840 | bytes 45385216 | tf_op jit(solution)/shard_map/rgk,ko->rgo/dot_general | solution.py:53
  69.5 3.1 copy.57
  72.6 4.3 fusion.172
  76.9 38.6 %all_to_all.15 = bf16[32,8,2048]{2,1,0:T(8,128)(2,1)S(1)} all-to-all(bf16[32,8,2048]{2,1,0:T(8,128)(2,1)S(1)} %get-tuple-element.17), channel_id=1, replica_groups=mesh['visit'=32,'tile'=8] {'visit'}, dimensions={0} | all-to-all | bytes 2097152 | tf_op jit(solution)/shard_map/all_to_all | solution.py:94
  115.5 4.6 %all-to-all-start.1 = ((bf16[32,8,2048]{2,1,0:T(8,128)(2,1)}), bf16[32,8,2048]{2,1,0:T(8,128)(2,1)S(1)}, u32[]{:S(2)}, u32[]{:S(2)}) async-start(bf16[32,8,2048]{2,1,0:T(8,128)(2,1)} %get-tuple-element.16), calls=%async_computation.1 | async-start | bytes 2097152 | tf_op jit(solution)/shard_map/all_to_all | solution.py:95
  121.4 27.4 %all-to-all-done.1 = bf16[32,8,2048]{2,1,0:T(8,128)(2,1)S(1)} async-done(((bf16[32,8,2048]{2,1,0:T(8,128)(2,1)}), bf16[32,8,2048]{2,1,0:T(8,128)(2,1)S(1)}, u32[]{:S(2)}, u32[]{:S(2)}) %all-to-all-start.1) | async-done | bytes 1048608 | tf_op jit(solution)/shard_map/all_to_all | solution.py:95
  150.1 4.3 stack.2
  154.5 5.2 %all-to-all-start.2 = ((bf16[32,8,8,2048]{3,2,1,0:T(8,128)(2,1)}), bf16[32,8,8,2048]{3,2,1,0:T(8,128)(2,1)}, u32[]{:S(2)}, u32[]{:S(2)}) async-start(bf16[32,8,8,2048]{3,2,1,0:T(8,128)(2,1)} %stack.2), calls=%async_computation.2 | async-start | bytes 16777216 | tf_op jit(solution)/shard_map/all_to_all | solution.py:104
  162.7 2.2 fusion.354
  165.7 193.5 %all-to-all-done.2 = bf16[32,8,8,2048]{3,2,1,0:T(8,128)(2,1)} async-done(((bf16[32,8,8,2048]{3,2,1,0:T(8,128)(2,1)}), bf16[32,8,8,2048]{3,2,1,0:T(8,128)(2,1)}, u32[]{:S(2)}, u32[]{:S(2)}) %all-to-all-start.2) | async-done | bytes 8388640 | tf_op jit(solution)/shard_map/all_to_all | solution.py:104
  359.2 8.3 %copy.282 = bf16[32,8,8,2048]{3,2,0,1:T(8,128)(2,1)} copy(bf16[32,8,8,2048]{3,2,1,0:T(8,128)(2,1)} %all-to-all-done.2) | data formatting | bytes 16777216 | tf_op jit(solution)/shard_map/all_to_all | solution.py:104
  370.4 2.7 collective-permute-start.3
  380.6 2.1 fusion.23
  382.6 2.1 fusion.26
  384.8 2.1 fusion.29
  386.9 2.1 fusion.32
  389.0 2.1 fusion.35
  391.1 2.2 fusion.38
  393.2 2.0 fusion.41
  395.3 2.1 fusion.44
  397.4 2.1 fusion.47
  399.4 2.1 fusion.50
  401.6 2.1 fusion.53
  403.7 2.1 fusion.56
  405.8 2.1 fusion.59
  407.9 2.2 fusion.62
  410.0 2.3 fusion.65
  412.3 2.1 fusion.68
  414.4 2.1 fusion.11
  416.5 14.4 %add_add_fusion = f32[256,16,128]{0,2,1:T(8,128)} fusion(f32[256,16,128]{0,2,1:T(8,128)} %fusion.11, f32[256,16,128]{0,2,1:T(8,128)} %fusion.68, f32[256,16,128]{0,2,1:T(8,128)} %fusion.65, f32[256,16,128]{0,2,1:T(8,128)} %fusion.62, f32[256,16,128]{0,2,1:T(8,128)} %fusion.59, f32[256,16,128]{0,2,1:T(8,128)} %fusion.56, f32[256,16,128]{0,2,1:T(8,128)} %fusion.53, ...), kind=kOutput, calls=%fused_computation.49 | convolution fusion | flops 168099840 | bytes 45385216 | tf_op jit(solution)/shard_map/rgk,ko->rgo/dot_general | solution.py:53
  (127 shorter events, 32.4 us)
Async XLA Ops:
  0.6 159.0 %copy-start = (s32[32,1]{0,1:T(1,128)S(1)}, s32[32,1]{0,1:T(1,128)}, u32[]{:S(2)}) copy-start(s32[32,1]{0,1:T(1,128)} %param.21) | copy-start | bytes 388
  1.5 13.5 %collective-permute-start = (bf16[10,2048]{1,0:T(8,128)(2,1)S(1)}, bf16[10,2048]{1,0:T(8,128)(2,1)S(1)}, u32[]{:S(2)}, u32[]{:S(2)}) collective-permute-start(bf16[10,2048]{1,0:T(8,128)(2,1)S(1)} %get-tuple-element.18), channel_id=1, source_target_pairs={{0,1},{1,2},{2,3},{3,4},{4,5},{5,6},{6,7},{8,9},{9,10},{10,11},{11... | collective-permute-start | bytes 122888 | tf_op jit(solution)/shard_map/ppermute | solution.py:16
  5.2 9.8 %collective-permute-start.1 = (bf16[10,2048]{1,0:T(8,128)(2,1)S(1)}, bf16[10,2048]{1,0:T(8,128)(2,1)S(1)}, u32[]{:S(2)}, u32[]{:S(2)}) collective-permute-start(bf16[10,2048]{1,0:T(8,128)(2,1)S(1)} %get-tuple-element.19), channel_id=1, source_target_pairs={{1,0},{2,1},{3,2},{4,3},{5,4},{6,5},{7,6},{9,8},{10,9},{11,10},{12... | collective-permute-start | bytes 122888 | tf_op jit(solution)/shard_map/ppermute | solution.py:19
  8.8 2.6 copy-start.3
  11.4 3.7 copy-start.4
  18.2 0.9 copy-start.41
  19.1 0.9 copy-start.40
  20.0 2.1 copy-start.39
  22.1 2.1 copy-start.38
  24.2 2.1 copy-start.37
  26.3 2.1 copy-start.36
  28.4 2.1 copy-start.35
  30.5 2.2 copy-start.34
  32.6 2.1 copy-start.33
  34.7 2.1 copy-start.32
  36.8 2.1 copy-start.31
  38.9 2.1 copy-start.30
  41.0 2.1 copy-start.29
  43.1 2.1 copy-start.28
  45.2 2.1 copy-start.26
  47.3 2.3 copy-start.24
  49.6 2.1 copy-start.7
  51.7 1.8 copy-start.6
  69.5 3.1 copy-start.2
  76.9 43.3 %copy-start.42 = (s32[32,1]{0,1:T(1,128)S(1)}, s32[32,1]{0,1:T(1,128)}, u32[]{:S(2)}) copy-start(s32[32,1]{0,1:T(1,128)} %param.18) | copy-start | bytes 388
  115.5 33.2 %all-to-all-start.1 = ((bf16[32,8,2048]{2,1,0:T(8,128)(2,1)}), bf16[32,8,2048]{2,1,0:T(8,128)(2,1)S(1)}, u32[]{:S(2)}, u32[]{:S(2)}) async-start(bf16[32,8,2048]{2,1,0:T(8,128)(2,1)} %get-tuple-element.16), calls=%async_computation.1 | async-start | bytes 2097152 | tf_op jit(solution)/shard_map/all_to_all | solution.py:95
  154.5 204.8 %all-to-all-start.2 = ((bf16[32,8,8,2048]{3,2,1,0:T(8,128)(2,1)}), bf16[32,8,8,2048]{3,2,1,0:T(8,128)(2,1)}, u32[]{:S(2)}, u32[]{:S(2)}) async-start(bf16[32,8,8,2048]{3,2,1,0:T(8,128)(2,1)} %stack.2), calls=%async_computation.2 | async-start | bytes 16777216 | tf_op jit(solution)/shard_map/all_to_all | solution.py:104
  368.4 6.0 %collective-permute-start.2 = (bf16[10,2048]{1,0:T(8,128)(2,1)S(1)}, bf16[10,2048]{1,0:T(8,128)(2,1)S(1)}, u32[]{:S(2)}, u32[]{:S(2)}) collective-permute-start(bf16[10,2048]{1,0:T(8,128)(2,1)S(1)} %get-tuple-element.14), channel_id=1, source_target_pairs={{0,1},{1,2},{2,3},{3,4},{4,5},{5,6},{6,7},{8,9},{9,10},{10,11},{11... | collective-permute-start | bytes 122888 | tf_op jit(solution)/shard_map/ppermute | solution.py:16
  370.4 5.6 %collective-permute-start.3 = (bf16[10,2048]{1,0:T(8,128)(2,1)S(1)}, bf16[10,2048]{1,0:T(8,128)(2,1)S(1)}, u32[]{:S(2)}, u32[]{:S(2)}) collective-permute-start(bf16[10,2048]{1,0:T(8,128)(2,1)S(1)} %get-tuple-element.15), channel_id=1, source_target_pairs={{1,0},{2,1},{3,2},{4,3},{5,4},{6,5},{7,6},{9,8},{10,9},{11,10},{12... | collective-permute-start | bytes 122888 | tf_op jit(solution)/shard_map/ppermute | solution.py:19
  378.8 0.9 copy-start.27
  380.6 2.1 copy-start.23
  382.6 2.1 copy-start.22
  384.8 2.1 copy-start.21
  386.9 2.1 copy-start.20
  389.0 2.1 copy-start.19
  391.1 2.2 copy-start.18
  393.2 2.1 copy-start.17
  395.3 2.1 copy-start.16
  397.3 2.1 copy-start.15
  399.4 2.1 copy-start.14
  401.6 2.1 copy-start.13
  403.7 2.1 copy-start.12
  405.8 2.1 copy-start.11
  407.9 2.2 copy-start.10
  410.0 2.3 copy-start.9
  412.3 2.1 copy-start.8
  430.9 2.0 copy-start.5
  430.9 3.6 copy-start.1
  (1 other events, 0.9 us)
